TPU v7x, 512 devices: a whole 4x4x16 slice. The times are simulated.
512 devices in a mesh: dp: 32 (over z_hi, x, core), proto: 16 (over z_lo, y).
Axes of the slice: x: 4, y: 4, z: 16 (z_hi: 4, z_lo: 4; z = z_hi * 4 + z_lo), core: 2. Of those that a mesh axis runs over, the one named last changes fastest.
Arguments:
- points: bfloat16 [65536, 768], P('dp'), may hold values from -6 to 6
- prototypes: bfloat16 [16384, 768], P('proto'), may hold values from -6 to 6
- plan_stride_lengths: float32 [3], replicated, may hold values from 1.5 to 5
- sigma_steps: float32 [3], replicated, may hold values from 0.2 to 1
Outputs:
- row_duals: float32 [65536], P('dp')
- col_duals: float32 [16384], P('proto')
- new_prototypes: float32 [16384, 768], P(('proto', 'dp'))
All inputs are finite; a program needn't handle non-finite values.
Results may differ from a plain program's by a relative error of at most 0.0017.
Values sent between devices are 32-bit elements; how exact they have to be, the bound alone decides.
A program may use at most 64 MiB of HBM per device.

v0:
```python
import jax
import jax.numpy as jnp
from jax import lax
from jax.sharding import PartitionSpec as P

K = 16384
ITERS = 3


sharpness_factor = 20.0


def unit_rows(values):
    wide = values.astype(jnp.float32)
    return (wide * lax.rsqrt(jnp.mean(wide * wide, axis=1, keepdims=True) + 1e-06)).astype(
        jnp.bfloat16
    )


def body(points, prototypes, plan_stride_lengths, sigma_steps):
    point_rows = points.shape[0]
    proto_rows = prototypes.shape[0]
    latent_dimension = prototypes.shape[1]
    col_target = float(point_rows * lax.axis_size("dp")) / K
    unit_points = unit_rows(points)
    unit_protos = unit_rows(prototypes)
    affinity_table = lax.dot_general(
        unit_points, unit_protos, (((1,), (1,)), ((), ())), preferred_element_type=jnp.float32
    )
    affinity_table = affinity_table * (sharpness_factor / latent_dimension)
    transport = jnp.zeros((point_rows, proto_rows), jnp.float32)
    row_duals = jnp.zeros((point_rows,), jnp.float32)
    col_duals = jnp.zeros((proto_rows,), jnp.float32)
    for step_index in range(ITERS):
        primal_step = plan_stride_lengths[step_index] / K
        fresh = jnp.maximum(
            0.0,
            transport - primal_step * (row_duals[:, None] + col_duals[None, :] - affinity_table),
        )
        extra = 2.0 * fresh - transport
        row_part = jnp.sum(extra, axis=1)
        col_part = jnp.sum(extra, axis=0)
        row_total = lax.psum(row_part, "proto")
        col_total = lax.psum(col_part, "dp")
        row_duals = row_duals + sigma_steps[step_index] * (row_total - 1.0)
        col_duals = col_duals + sigma_steps[step_index] * (col_total - col_target)
        transport = fresh
    counts = lax.psum(jnp.sum(transport, axis=0), "dp")
    plan_low = transport.astype(jnp.bfloat16)
    out_rows = proto_rows // lax.axis_size("dp")
    first_row = lax.axis_index("dp") * out_rows
    local_sum = lax.dot_general(
        plan_low, points, (((0,), (0,)), ((), ())), preferred_element_type=jnp.float32
    )
    whole_sum = lax.psum(local_sum, "dp")
    gathered = lax.dynamic_slice_in_dim(whole_sum, first_row, out_rows, 0)
    my_counts = lax.dynamic_slice_in_dim(counts, first_row, out_rows, 0)
    previous = lax.dynamic_slice_in_dim(prototypes, first_row, out_rows, 0).astype(jnp.float32)
    new_prototypes = (previous + gathered) / (1.0 + my_counts)[:, None]
    return (row_duals, col_duals, new_prototypes)


def solution(mesh):
    placed = (P("dp", None), P("proto", None), P(), P())
    return jax.shard_map(
        body,
        mesh=mesh,
        in_specs=placed,
        out_specs=(P("dp"), P("proto"), P(("proto", "dp"), None)),
        check_vma=False,
    )
```

profile of v0, /device:TPU:1, one launch (start us, length us, event | category | flops | bytes accessed | tf_op | source)
XLA Modules:
  0.0 678.3 jit_solution(16469381388283278491)
XLA Ops:
  7.2 0.0 all-reduce.3.cloned.1.call-start
  7.2 1.4 fusion.18
  8.6 1.8 fusion.7
  10.4 2.6 fusion.1
  13.6 0.0 copy-start.1
  13.6 10.5 %fusion.3 = (f32[1024]{0:T(1024)S(1)}, f32[2048]{0:T(1024)S(1)}, f32[2048,1024]{1,0:T(8,128)}) fusion(f32[]{:T(128)} %bitcast.1, bf16[1024,768]{1,0:T(8,128)(2,1)} %param.5, f32[1024]{0:T(1024)S(1)} %add_rsqrt_fusion.1, bf16[2048,768]{1,0:T(8,128)(2,1)} %param.4, f32[2048]{0:T(1024)S(1)} %add_rsqrt_fusion), kind=kOutput, calls=%fused_computation.10 | convolution fusion | flops 3245077504 | bytes 13131780 | tf_op jit(solution)/shard_map/dot_general | solution.py:27
  24.1 0.0 copy-start
  24.1 90.7 %psum.57 = f32[1024]{0:T(1024)S(1)} all-reduce(f32[1024]{0:T(1024)S(1)} %get-tuple-element.7), channel_id=1, replica_groups=mesh['dp'=32,'proto'=16] {'dp'}, use_global_device_ids=true, to_apply=%region_5.0 | all-reduce | flops 1024 | bytes 8192 | tf_op jit(solution)/shard_map/psum | solution.py:44
  114.8 0.0 copy-done.1
  114.8 0.6 fusion.17
  115.5 35.4 %psum.56 = f32[2048]{0:T(1024)S(1)} all-reduce(f32[2048]{0:T(1024)S(1)} %get-tuple-element.8), channel_id=1, replica_groups=mesh['dp'=32,'proto'=16] {'proto'}, use_global_device_ids=true, to_apply=%region_3.0 | all-reduce | flops 2048 | bytes 16384 | tf_op jit(solution)/shard_map/psum | solution.py:43
  150.9 0.6 add_multiply_fusion.1
  151.5 0.6 add_multiply_fusion
  152.7 6.8 fusion.16
  159.5 31.4 %psum.58 = f32[2048]{0:T(1024)S(1)} all-reduce(f32[2048]{0:T(1024)S(1)} %get-tuple-element.6), channel_id=1, replica_groups=mesh['dp'=32,'proto'=16] {'proto'}, use_global_device_ids=true, to_apply=%region_7.0 | all-reduce | flops 2048 | bytes 16384 | tf_op jit(solution)/shard_map/psum | solution.py:43
  190.9 105.7 %psum.59 = f32[1024]{0:T(1024)S(1)} all-reduce(f32[1024]{0:T(1024)S(1)} %get-tuple-element.5), channel_id=1, replica_groups=mesh['dp'=32,'proto'=16] {'dp'}, use_global_device_ids=true, to_apply=%region_9.0 | all-reduce | flops 1024 | bytes 8192 | tf_op jit(solution)/shard_map/psum | solution.py:44
  296.6 1.2 multiply_add_fusion.1
  297.8 1.2 multiply_add_fusion.3
  299.6 0.0 copy-done
  299.6 11.3 %fusion.5 = f32[1024,768]{1,0:T(8,128)} fusion(bf16[2048,768]{1,0:T(8,128)(2,1)S(1)} %copy-done, f32[2048,1024]{1,0:T(8,128)} %get-tuple-element.19, f32[1024]{0:T(1024)S(1)} %multiply_add_fusion.3, f32[2048]{0:T(1024)S(1)} %multiply_add_fusion.1, f32[]{:T(128)} %bitcast.5, f32[1024]{0:T(1024)S(1)} %add_multiply_fusion.1, f32[2048]{0:T(1024)S(1)} %add_multiply_fusion, ...), kind=kOutput, calls=%fused_computation.12 | convolution fusion | flops 3254779904 | bytes 14704652 | tf_op jit(solution)/shard_map/dot_general | solution.py:52
  311.0 0.0 all-reduce.3.cloned.1.call-update
  311.0 8.7 %fusion.14 = (f32[1024]{0:T(1024)S(1)}, f32[2048,1024]{1,0:T(8,128)S(1)}) fusion(f32[1024]{0:T(1024)S(1)} %multiply_add_fusion.3, f32[2048]{0:T(1024)S(1)} %multiply_add_fusion.1, f32[]{:T(128)} %bitcast.5, f32[1024]{0:T(1024)S(1)} %add_multiply_fusion.1, f32[2048]{0:T(1024)S(1)} %add_multiply_fusion, f32[]{:T(128)} %bitcast.3, ...), kind=kLoop, calls=%fused_computation.31 | loop fusion | flops 37747712 | bytes 16805900 | tf_op jit(solution)/shard_map/reduce_sum | solution.py:48
  319.7 0.7 fusion.15
  320.4 88.4 %all-reduce = (f32[1024]{0:T(1024)S(1)}, f32[1024]{0:T(1024)S(1)}) all-reduce(f32[1024]{0:T(1024)S(1)} %get-tuple-element.3, f32[1024]{0:T(1024)S(1)} %get-tuple-element.11), channel_id=1, replica_groups=mesh['dp'=32,'proto'=16] {'dp'}, use_global_device_ids=true, to_apply=%region_13.0 | all-reduce | flops 2048 | bytes 16384 | tf_op jit(solution)/shard_map/psum | solution.py:44
  408.8 34.8 %psum.60 = f32[2048]{0:T(1024)S(1)} all-reduce(f32[2048]{0:T(1024)S(1)} %get-tuple-element.4), channel_id=1, replica_groups=mesh['dp'=32,'proto'=16] {'proto'}, use_global_device_ids=true, to_apply=%region_11.0 | all-reduce | flops 2048 | bytes 16384 | tf_op jit(solution)/shard_map/psum | solution.py:43
  443.6 0.1 dynamic-slice_add_fusion
  443.6 1.2 multiply_add_fusion.2
  444.9 1.2 multiply_add_fusion
  446.1 223.8 %all-reduce.3.cloned.1.call-done = f32[1024,768]{1,0:T(8,128)} async-done(((f32[1024,768]{1,0:T(8,128)}), f32[1024,768]{1,0:T(8,128)}) %all-reduce.3.cloned.1.call-update) | async-done | bytes 3145744 | tf_op jit(solution)/shard_map/psum | solution.py:55
  669.9 1.6 add_divide_fusion
  (2 shorter events, 0.0 us)
Async XLA Ops:
  7.2 662.7 %all-reduce.3.cloned.1.call-start = ((), (), s32[]{:S(2)}) async-start(), calls=%async_computation | async-start | bytes 6291456 | tf_op jit(solution)/shard_map/psum | solution.py:55
  13.6 101.2 %copy-start.1 = (f32[3]{0:T(128)S(1)}, f32[3]{0:T(128)}, u32[]{:S(2)}) copy-start(f32[3]{0:T(128)} %param.7) | copy-start | bytes 40
  24.1 275.5 %copy-start = (bf16[2048,768]{1,0:T(8,128)(2,1)S(1)}, bf16[2048,768]{1,0:T(8,128)(2,1)}, u32[]{:S(2)}) copy-start(bf16[2048,768]{1,0:T(8,128)(2,1)} %param.4) | copy-start | bytes 9437188
Sparse Core Ops, SparseCore 0:
  311.1 358.7 all-reduce.2
where the time goes:
time: 681 us; the launch traced here: 678 us
  blocking collectives  386 us (57%)
  waiting for transfers between devices  224 us (33%)
  other arithmetic  28.2 us (4%)
  matrix products  21.8 us (3%)
  between operations  16.1 us (2%)
    psum x3, blocking collectives, body(): col_total = lax.psum(col_part, 'dp')  285 us
    psum x1, waiting for transfers between devices, body(): whole_sum = lax.psum(local_sum, 'dp')  224 us
    psum x3, blocking collectives, body(): row_total = lax.psum(row_part, 'proto')  102 us
  transfers between devices with their start and end apart: 1, of which 1 were waited for; matrix products, arithmetic and copies ran while one was open for 2% of the time, Pallas kernels for 0%

commit v1 on v0

v1 whole, which is shorter than its diff:
```python
import jax
import jax.numpy as jnp
from jax import lax
from jax.experimental import pallas as pl
from jax.experimental.pallas import tpu as pltpu
from jax.sharding import PartitionSpec as P

K = 16384
SHARPNESS = 20.0
MESH = pl.DeviceIdType.MESH

ZH, X, CORE, ZL, Y = 4, 4, 2, 4, 4
ROUNDS = 3
POINTS, PROTOS, WIDTH = 2048, 1024, 768
PCHUNK = 256
NCHUNK = POINTS // PCHUNK
LANES = POINTS // 128
GROUPS = PROTOS // 8
BLOCK = PROTOS // ZH
BGROUPS = BLOCK // 8
OUT = PROTOS // (ZH * X * CORE)
HALF = OUT // 2
ORDER = (2, 1, 3, 0)
F32, BF16 = jnp.float32, jnp.bfloat16


def unit_rows(values):
    wide = values.astype(F32)
    return (wide * lax.rsqrt(jnp.mean(wide * wide, axis=1, keepdims=True) + 1e-06)).astype(BF16)


def kernel(
    strides, sigmas, pts_hbm, protos_hbm,
    rowd_ref, cold_ref, newp_ref,
    pts, protos, uprot, a_ref, b_ref, plan, wr, wc, rowacc, colacc,
    ra, rb, ca, cb, part, corebuf, xmid, xend, total, zmid, zend, count_ref,
    in_sem, ra_s, ra_r, rb_s, rb_r, ca_s, ca_r, cb_s, cb_r, core_s, core_r, x_s, x_r, z_s, z_r,
):
    me_dp, me_pr = lax.axis_index("dp"), lax.axis_index("proto")
    zh, x, core = me_dp // (X * CORE), (me_dp // CORE) % X, me_dp % CORE
    xc = me_dp % (X * CORE)
    zl, y = me_pr // Y, me_pr % Y

    def at_xc(d):
        return (zh * (X * CORE) + d, me_pr)

    def at_x(d):
        return at_xc(((x + d + X) % X) * CORE + core)

    def at_zh(d):
        return (((zh + d + ZH) % ZH) * (X * CORE) + xc, me_pr)

    def at_y(d):
        return (me_dp, zl * Y + (y + d) % Y)

    def at_zl(d):
        return (me_dp, ((zl + d) % ZL) * Y + y)

    xc_peers = []
    for d in range(1, X * CORE):
        slot = ((x + d // CORE) % X) * CORE + (core + d % CORE) % CORE
        xc_peers.append((slot, at_xc(slot)))
    zh_peers = [((zh + d) % ZH, at_zh(d)) for d in range(1, ZH)]
    y_peers = [((y + d) % Y, at_y(d)) for d in range(1, Y)]
    zl_peers = [((zl + d) % ZL, at_zl(d)) for d in range(1, ZL)]
    everyone = xc_peers + zh_peers + y_peers + zl_peers

    barrier = pltpu.get_barrier_semaphore()
    for _, dev in everyone:
        pl.semaphore_signal(barrier, inc=1, device_id=dev, device_id_type=MESH)

    protos_in = pltpu.make_async_copy(protos_hbm, protos, in_sem.at[NCHUNK])
    protos_in.start()

    def pts_in(j):
        rows = pl.ds(j * PCHUNK, PCHUNK)
        return pltpu.make_async_copy(pts_hbm.at[rows], pts.at[rows], in_sem.at[j])

    for j in range(NCHUNK):
        pts_in(j).start()

    scale = SHARPNESS / WIDTH
    tau = [strides[t] / K for t in range(ROUNDS)]
    target = float(POINTS * ZH * X * CORE) / K

    pending = []

    def spread(buf, send, recv, t, mine, peers):
        for slot, dev in peers:
            copy = pltpu.make_async_remote_copy(
                src_ref=buf.at[t, mine], dst_ref=buf.at[t, mine],
                send_sem=send.at[t, slot], recv_sem=recv.at[t, mine],
                device_id=dev, device_id_type=MESH)
            copy.start()
            pending.append(copy)

    def gather(buf, send, recv, t, peers):
        for slot, dev in peers:
            pltpu.make_async_remote_copy(
                src_ref=buf.at[t, slot], dst_ref=buf.at[t, slot],
                send_sem=send.at[t, slot], recv_sem=recv.at[t, slot],
                device_id=dev, device_id_type=MESH).wait_recv()
        out = buf[t, 0]
        for slot in range(1, buf.shape[1]):
            out = out + buf[t, slot]
        return out

    def sums_out(t, factor):
        for g in range(PROTOS // 128):
            block = colacc[g * 16:(g + 1) * 16].reshape(128, 128)
            ca[t, xc, g:g + 1, :] = factor * jnp.sum(block.T, axis=0, keepdims=True)
        spread(ca, ca_s, ca_r, t, xc, xc_peers)
        for l in range(LANES):
            ra[t, y, l:l + 1, :] = factor * jnp.sum(rowacc[:, l * 128:(l + 1) * 128], axis=0, keepdims=True)
        spread(ra, ra_s, ra_r, t, y, y_peers)

    def sums_mid(t):
        cb[t, zh] = gather(ca, ca_s, ca_r, t, xc_peers)
        spread(cb, cb_s, cb_r, t, zh, zh_peers)
        rb[t, zl] = gather(ra, ra_s, ra_r, t, y_peers)
        spread(rb, rb_s, rb_r, t, zl, zl_peers)

    def sums_in(t):
        cols = gather(cb, cb_s, cb_r, t, zh_peers)
        rows = gather(rb, rb_s, rb_r, t, zl_peers)
        return rows, cols

    def duals_in(rowd, cold, step):
        tall = (step * cold).T
        for g in range(PROTOS // 128):
            wc[g * 16:(g + 1) * 16] = jnp.broadcast_to(tall[:, g:g + 1], (128, 128)).reshape(16, 8, 128)
        for l in range(LANES):
            wr[:, l * 128:(l + 1) * 128] = jnp.broadcast_to(step * rowd[l:l + 1, :], (8, 128))

    protos_in.wait()

    def unit_protos(i, carry):
        rows = pl.ds(pl.multiple_of(i * 128, 128), 128)
        uprot[rows, :] = unit_rows(protos[rows, :])
        return carry

    lax.fori_loop(0, PROTOS // 128, unit_protos, 0)
    colacc[...] = jnp.zeros_like(colacc)

    def scores(j, carry):
        pts_in(j).wait()
        first = pl.multiple_of(j * PCHUNK, PCHUNK)
        unit = unit_rows(pts[pl.ds(first, PCHUNK), :])
        s = lax.dot_general(uprot[...], unit, (((1,), (1,)), ((), ())), preferred_element_type=F32)
        s = s.reshape(GROUPS, 8, PCHUNK)
        a_ref[:, :, pl.ds(first, PCHUNK)] = s
        p = jnp.maximum(s, 0.0)
        rowacc[:, pl.ds(first, PCHUNK)] = jnp.sum(p, axis=0)
        part_sum = p[:, :, 0:128]
        for l in range(1, PCHUNK // 128):
            part_sum = part_sum + p[:, :, l * 128:(l + 1) * 128]
        colacc[...] += part_sum
        return carry

    lax.fori_loop(0, NCHUNK, scores, 0)
    pl.semaphore_wait(barrier, len(everyone))

    def first_plan(i, carry):
        rows = pl.ds(i * 4, 4)
        s = a_ref[rows]
        b_ref[rows] = jnp.maximum((tau[1] * scale) * s, ((tau[0] + tau[1]) * scale) * s)
        return carry

    def next_plan(i, carry):
        rows = pl.ds(i * 4, 4)
        b_ref[rows] = b_ref[rows] + (tau[2] * scale) * a_ref[rows]
        return carry

    def iterate(base, count, store):
        def step(i, carry):
            rows = pl.ds(base + i * 4, 4)
            c = wc[rows]
            acc = None
            for l in range(LANES):
                lanes = slice(l * 128, (l + 1) * 128)
                p = jnp.maximum(b_ref[rows, :, lanes] - (wr[:, lanes] + c), 0.0)
                rowacc[:, lanes] += jnp.sum(p, axis=0)
                acc = p if acc is None else acc + p
                store(i, rows, lanes, p)
            colacc[rows] = acc
            return carry

        lax.fori_loop(0, count, step, 0)

    sums_out(0, tau[0] * scale)
    lax.fori_loop(0, GROUPS // 8, first_plan, 0)
    sums_mid(0)
    lax.fori_loop(GROUPS // 8, GROUPS // 4, first_plan, 0)
    rows1, cols1 = sums_in(0)
    rowd = sigmas[0] * (2.0 * rows1 - 1.0)
    cold = sigmas[0] * (2.0 * cols1 - target)
    duals_in(rowd, cold, tau[1])

    rowacc[...] = jnp.zeros_like(rowacc)

    def keep(i, rows, lanes, p):
        b_ref[rows, :, lanes] = p

    iterate(0, GROUPS // 4, keep)
    sums_out(1, 1.0)
    lax.fori_loop(0, GROUPS // 8, next_plan, 0)
    sums_mid(1)
    lax.fori_loop(GROUPS // 8, GROUPS // 4, next_plan, 0)
    rows2, cols2 = sums_in(1)
    rowd = rowd + sigmas[1] * (2.0 * rows2 - rows1 - 1.0)
    cold = cold + sigmas[1] * (2.0 * cols2 - cols1 - target)
    duals_in(rowd, cold, tau[2])

    rowacc[...] = jnp.zeros_like(rowacc)
    other = 1 - core

    def remote(src, dst, sems, index, dev):
        return pltpu.make_async_remote_copy(
            src_ref=src, dst_ref=dst, send_sem=sems[0].at[index], recv_sem=sems[1].at[index],
            device_id=dev, device_id_type=MESH)

    core_sems, x_sems, z_sems = (core_s, core_r), (x_s, x_r), (z_s, z_r)
    peer = at_xc(x * CORE + other)

    def go(copy):
        copy.start()
        pending.append(copy)
        return copy

    def compute(c):
        base = ((zh + ORDER[c]) % ZH) * BGROUPS

        def low(i, rows, lanes, p):
            plan[pl.ds(pl.multiple_of(i * 32, 32), 32), lanes] = p.reshape(32, 128).astype(BF16)

        iterate(base, BGROUPS // 4, low)
        for n in range(WIDTH // 256):
            lanes = slice(n * 256, (n + 1) * 256)
            g = jnp.dot(plan[...], pts[:, lanes], preferred_element_type=F32)
            part[c, :, :, :, lanes] = g.reshape(X, CORE, OUT, 256)
        return go(remote(part.at[c, :, other], corebuf.at[c], core_sems, c, peer))

    right, left = at_x(1), at_x(-1)
    up, down = at_zh(1), at_zh(-1)
    xp, xm, xo = (x + 1) % X, (x + X - 1) % X, (x + 2) % X
    lo, hi = pl.ds(0, HALF), pl.ds(HALF, HALF)

    def x_first(c, core_copy):
        core_copy.wait_recv()
        part[c, xo, core] += corebuf[c, xo]
        far = [
            go(remote(part.at[c, xo, core, lo], xmid.at[c, 0], x_sems, (c, 0), right)),
            go(remote(part.at[c, xo, core, hi], xmid.at[c, 1], x_sems, (c, 1), left)),
        ]
        part[c, xp, core] += corebuf[c, xp]
        part[c, xm, core] += corebuf[c, xm]
        near = [
            go(remote(part.at[c, xp, core, hi], xend.at[c, 0, hi], x_sems, (c, 2), right)),
            go(remote(part.at[c, xm, core, lo], xend.at[c, 1, lo], x_sems, (c, 3), left)),
        ]
        part[c, x, core] += corebuf[c, x]
        return far, near

    def x_second(c, copies):
        far, near = copies
        far[0].wait_recv()
        part[c, xp, core, lo] += xmid[c, 0]
        near.append(go(remote(part.at[c, xp, core, lo], xend.at[c, 0, lo], x_sems, (c, 4), right)))
        far[1].wait_recv()
        part[c, xm, core, hi] += xmid[c, 1]
        near.append(go(remote(part.at[c, xm, core, hi], xend.at[c, 1, hi], x_sems, (c, 5), left)))
        return near

    def x_last(c, near):
        for copy in near:
            copy.wait_recv()
        total[c] = part[c, x, core] + xend[c, 0] + xend[c, 1]

    k0 = compute(0)
    k1 = compute(1)
    x0 = x_first(0, k0)
    k2 = compute(2)
    x1 = x_first(1, k1)
    x0 = x_second(0, x0)
    k3 = compute(3)
    x2 = x_first(2, k2)
    sums_out(2, 1.0)
    x1 = x_second(1, x1)
    x3 = x_first(3, k3)
    x_last(0, x0)
    zfar = [
        go(remote(total.at[0, lo], zmid.at[0], z_sems, 0, up)),
        go(remote(total.at[0, hi], zmid.at[1], z_sems, 1, down)),
    ]
    sums_mid(2)
    x2 = x_second(2, x2)
    x_last(1, x1)
    znear = [go(remote(total.at[1, hi], zend.at[0, hi], z_sems, 2, up))]
    x3 = x_second(3, x3)
    x_last(2, x2)
    znear.append(go(remote(total.at[2, lo], zend.at[1, lo], z_sems, 3, down)))
    zfar[0].wait_recv()
    total[1, lo] += zmid[0]
    znear.append(go(remote(total.at[1, lo], zend.at[0, lo], z_sems, 4, up)))
    zfar[1].wait_recv()
    total[2, hi] += zmid[1]
    znear.append(go(remote(total.at[2, hi], zend.at[1, hi], z_sems, 5, down)))
    rows3, cols3 = sums_in(2)
    rowd_ref[...] = rowd + sigmas[2] * (2.0 * rows3 - rows2 - 1.0)
    cold_ref[...] = cold + sigmas[2] * (2.0 * cols3 - cols2 - target)
    count_ref[...] = cols3
    mine = count_ref[pl.ds(me_dp // 4, 1), :]
    sub = lax.broadcasted_iota(jnp.int32, (OUT, 128), 0)
    lane = lax.broadcasted_iota(jnp.int32, (OUT, 128), 1)
    counts = jnp.sum(jnp.where(lane == sub + (me_dp % 4) * OUT, mine, 0.0), axis=1, keepdims=True)
    previous = protos[pl.ds(pl.multiple_of(me_dp * OUT, OUT), OUT), :].astype(F32)
    x_last(3, x3)
    for copy in znear:
        copy.wait_recv()
    gathered = total[3] + zend[0] + zend[1]
    newp_ref[...] = (previous + gathered) / (1.0 + counts)
    for copy in pending:
        copy.wait_send()


def body(points, prototypes, plan_stride_lengths, sigma_steps):
    dma = pltpu.SemaphoreType.DMA
    vmem = pl.BlockSpec(memory_space=pltpu.VMEM)
    smem = pl.BlockSpec(memory_space=pltpu.SMEM)
    hbm = pl.BlockSpec(memory_space=pl.ANY)
    rows, cols, new = pl.pallas_call(
        kernel,
        out_shape=(
            jax.ShapeDtypeStruct((LANES, 128), F32),
            jax.ShapeDtypeStruct((PROTOS // 128, 128), F32),
            jax.ShapeDtypeStruct((OUT, WIDTH), F32),
        ),
        in_specs=[smem, smem, hbm, hbm],
        out_specs=(vmem, vmem, vmem),
        scratch_shapes=[
            pltpu.VMEM((POINTS, WIDTH), BF16),
            pltpu.VMEM((PROTOS, WIDTH), BF16),
            pltpu.VMEM((PROTOS, WIDTH), BF16),
            pltpu.VMEM((GROUPS, 8, POINTS), F32),
            pltpu.VMEM((GROUPS, 8, POINTS), F32),
            pltpu.VMEM((BLOCK, POINTS), BF16),
            pltpu.VMEM((8, POINTS), F32),
            pltpu.VMEM((GROUPS, 8, 128), F32),
            pltpu.VMEM((8, POINTS), F32),
            pltpu.VMEM((GROUPS, 8, 128), F32),
            pltpu.VMEM((ROUNDS, Y, LANES, 128), F32),
            pltpu.VMEM((ROUNDS, ZL, LANES, 128), F32),
            pltpu.VMEM((ROUNDS, X * CORE, PROTOS // 128, 128), F32),
            pltpu.VMEM((ROUNDS, ZH, PROTOS // 128, 128), F32),
            pltpu.VMEM((ZH, X, CORE, OUT, WIDTH), F32),
            pltpu.VMEM((ZH, X, OUT, WIDTH), F32),
            pltpu.VMEM((ZH, 2, HALF, WIDTH), F32),
            pltpu.VMEM((ZH, 2, OUT, WIDTH), F32),
            pltpu.VMEM((ZH, OUT, WIDTH), F32),
            pltpu.VMEM((2, HALF, WIDTH), F32),
            pltpu.VMEM((2, OUT, WIDTH), F32),
            pltpu.VMEM((PROTOS // 128, 128), F32),
            dma((NCHUNK + 1,)),
            dma((ROUNDS, Y)), dma((ROUNDS, Y)),
            dma((ROUNDS, ZL)), dma((ROUNDS, ZL)),
            dma((ROUNDS, X * CORE)), dma((ROUNDS, X * CORE)),
            dma((ROUNDS, ZH)), dma((ROUNDS, ZH)),
            dma((ZH,)), dma((ZH,)),
            dma((ZH, 6)), dma((ZH, 6)),
            dma((6,)), dma((6,)),
        ],
        compiler_params=pltpu.CompilerParams(
            collective_id=0, has_side_effects=True, vmem_limit_bytes=56 * 1024 * 1024),
        name="assign",
    )(plan_stride_lengths, sigma_steps, points, prototypes)
    return rows.reshape(POINTS), cols.reshape(PROTOS), new


def solution(mesh):
    placed = (P("dp", None), P("proto", None), P(), P())
    return jax.shard_map(
        body,
        mesh=mesh,
        in_specs=placed,
        out_specs=(P("dp"), P("proto"), P(("proto", "dp"), None)),
        check_vma=False,
    )
```

time: 681 us -> 80.3 us (0.12)
  blocking collectives: 386 us -> 0 us
  waiting for transfers between devices: 224 us -> 0 us
  Pallas kernels: 0 us -> 75.3 us
  other arithmetic: 28.2 us -> 0 us
  matrix products: 21.8 us -> 0 us
  between operations: 16.1 us -> 0.64 us
    psum x6 -> x0, blocking collectives: 386 us -> none  [the longest x3 285 us: body(): col_total = lax.psum(col_part, 'dp')]
    psum x1 -> x0, waiting for transfers between devices: 224 us -> none  [body(): whole_sum = lax.psum(local_sum, 'dp')]
    pallas_call x0 -> x1, Pallas kernels: none -> 75.3 us  [body(): pl.pallas_call(kernel, out_shape=(jax.ShapeDtypeStruct((LANES, 128), F32)...]
    dot_general x2 -> x0, matrix products: 21.8 us -> none  [the longest x1 11.3 us: body(): lax.dot_general(plan_low, points, (((0,), (0,)), ((), ())), preferred_ele...]
    reduce_sum x5 -> x0, other arithmetic: 20.5 us -> none  [the longest x1 8.67 us: body(): counts = lax.psum(jnp.sum(transport, axis=0), 'dp')]
  transfers between devices with their start and end apart: 1 -> 0, of which waited for: 1 -> 0; matrix products, arithmetic and copies ran while one was open for 2% -> 0% of each run, Pallas kernels for 0% -> 0%
where the time goes in v1:
time: 80.3 us; the launch traced here: 80 us
  Pallas kernels  75.3 us (94%)
  local copies, waits for them, and re-layouts  4.1 us (5%)
    pallas_call x1, Pallas kernels, body(): pl.pallas_call(kernel, out_shape=(jax.ShapeDtypeStruct((LANES, 128), F32)...  75.3 us
    unnamed x3, local copies, waits for them, and re-layouts  4.1 us

profile of v1, /device:TPU:1, one launch (start us, length us, event | category | flops | bytes accessed | tf_op | source)
XLA Modules:
  0.0 80.0 jit_solution(404312158016108285)
XLA Ops:
  0.6 75.3 %assign.1 = (f32[16,128]{1,0:T(8,128)}, f32[8,128]{1,0:T(8,128)}, f32[32,768]{1,0:T(8,128)}) custom-call(f32[3]{0:T(128)} %strides.1, f32[3]{0:T(128)} %sigmas.1, bf16[2048,768]{1,0:T(8,128)(2,1)} %pts_hbm.1, bf16[1024,768]{1,0:T(8,128)(2,1)} %protos_hbm.1), custom_call_target="tpu_custom_call" | custom-call | tf_op jit(solution)/shard_map/assign/pallas_call | solution.py:331
  75.9 1.3 %copy.10 = f32[2048]{0:T(1024)} copy(f32[2048]{0:T(1024)} %bitcast.2) | data formatting | bytes 16384
  77.2 1.3 %copy.11 = f32[1024]{0:T(1024)} copy(f32[1024]{0:T(1024)} %bitcast.3) | data formatting | bytes 8192
  78.5 1.5 %copy.12 = f32[32,768]{1,0:T(8,128)} copy(f32[32,768]{1,0:T(8,128)} %get-tuple-element.14) | data formatting | bytes 196608

commit v2 on v1

v2 whole, which is shorter than its diff:
```python
import jax
import jax.numpy as jnp
from jax import lax
from jax.experimental import pallas as pl
from jax.experimental.pallas import tpu as pltpu
from jax.sharding import PartitionSpec as P

K = 16384
SHARPNESS = 20.0
MESH = pl.DeviceIdType.MESH

ZH, X, CORE, ZL, Y = 4, 4, 2, 4, 4
ROUNDS = 3
POINTS, PROTOS, WIDTH = 2048, 1024, 768
PCHUNK = 512
NCHUNK = POINTS // PCHUNK
PHALF = PROTOS // 2
LANES = POINTS // 128
GROUPS = PROTOS // 8
BLOCK = PROTOS // ZH
BGROUPS = BLOCK // 8
OUT = PROTOS // (ZH * X * CORE)
HALF = OUT // 2
THIRDS = WIDTH // 256
F32, BF16 = jnp.float32, jnp.bfloat16


def unit_rows(values):
    wide = values.astype(F32)
    return (wide * lax.rsqrt(jnp.mean(wide * wide, axis=1, keepdims=True) + 1e-06)).astype(BF16)


def kernel(
    strides_hbm, sigmas_hbm, pts_hbm, protos_hbm,
    rowd_ref, cold_ref, newp_ref,
    strides, sigmas, pts, protos, upts, uprot, a_ref, b_ref, plan, wr, wc, rowacc, colacc,
    ra, rb, ca, cb, part, corebuf, xbuf, total, zmid, zend, count_ref,
    in_sem, ra_s, ra_r, rb_s, rb_r, ca_s, ca_r, cb_s, cb_r, core_s, core_r, x_s, x_r, far_s, far_r, near_s, near_r,
):
    me_dp, me_pr = lax.axis_index("dp"), lax.axis_index("proto")
    zh, x, core = me_dp // (X * CORE), (me_dp // CORE) % X, me_dp % CORE
    xc = me_dp % (X * CORE)
    zl, y = me_pr // Y, me_pr % Y

    def at_xc(d):
        return (zh * (X * CORE) + d, me_pr)

    def at_x(d):
        return at_xc(((x + d + X) % X) * CORE + core)

    def at_zh(d):
        return (((zh + d + ZH) % ZH) * (X * CORE) + xc, me_pr)

    def at_y(d):
        return (me_dp, zl * Y + (y + d) % Y)

    def at_zl(d):
        return (me_dp, ((zl + d) % ZL) * Y + y)

    xc_peers = []
    for d in range(1, X * CORE):
        slot = ((x + d // CORE) % X) * CORE + (core + d % CORE) % CORE
        xc_peers.append((slot, at_xc(slot)))
    zh_peers = [((zh + d) % ZH, at_zh(d)) for d in range(1, ZH)]
    y_peers = [((y + d) % Y, at_y(d)) for d in range(1, Y)]
    zl_peers = [((zl + d) % ZL, at_zl(d)) for d in range(1, ZL)]
    everyone = xc_peers + zh_peers + y_peers + zl_peers

    barrier = pltpu.get_barrier_semaphore()
    for _, dev in everyone:
        pl.semaphore_signal(barrier, inc=1, device_id=dev, device_id_type=MESH)

    def protos_in(h):
        rows = pl.ds(h * PHALF, PHALF)
        return pltpu.make_async_copy(protos_hbm.at[rows], protos.at[rows], in_sem.at[NCHUNK + h])

    def pts_in(j):
        rows = pl.ds(j * PCHUNK, PCHUNK)
        return pltpu.make_async_copy(pts_hbm.at[rows], pts.at[rows], in_sem.at[j])

    protos_in(0).start()
    for j in range(NCHUNK):
        pts_in(j).start()
    protos_in(1).start()
    strides_in = pltpu.make_async_copy(strides_hbm, strides, in_sem.at[NCHUNK + 2])
    sigmas_in = pltpu.make_async_copy(sigmas_hbm, sigmas, in_sem.at[NCHUNK + 3])
    strides_in.start()
    sigmas_in.start()

    scale = SHARPNESS / WIDTH
    target = float(POINTS * ZH * X * CORE) / K

    pending = []

    def spread(buf, send, recv, t, mine, peers):
        for slot, dev in peers:
            copy = pltpu.make_async_remote_copy(
                src_ref=buf.at[t, mine], dst_ref=buf.at[t, mine],
                send_sem=send.at[t, slot], recv_sem=recv.at[t, mine],
                device_id=dev, device_id_type=MESH)
            copy.start()
            pending.append(copy)

    def gather(buf, send, recv, t, peers):
        for slot, dev in peers:
            pltpu.make_async_remote_copy(
                src_ref=buf.at[t, slot], dst_ref=buf.at[t, slot],
                send_sem=send.at[t, slot], recv_sem=recv.at[t, slot],
                device_id=dev, device_id_type=MESH).wait_recv()
        out = buf[t, 0]
        for slot in range(1, buf.shape[1]):
            out = out + buf[t, slot]
        return out

    def sums_out(t, factor):
        for g in range(PROTOS // 128):
            block = colacc[g * 16:(g + 1) * 16].reshape(128, 128)
            ca[t, xc, g:g + 1, :] = factor * jnp.sum(block.T, axis=0, keepdims=True)
        spread(ca, ca_s, ca_r, t, xc, xc_peers)
        for l in range(LANES):
            ra[t, y, l:l + 1, :] = factor * jnp.sum(rowacc[:, l * 128:(l + 1) * 128], axis=0, keepdims=True)
        spread(ra, ra_s, ra_r, t, y, y_peers)

    def sums_mid(t):
        cb[t, zh] = gather(ca, ca_s, ca_r, t, xc_peers)
        spread(cb, cb_s, cb_r, t, zh, zh_peers)
        rb[t, zl] = gather(ra, ra_s, ra_r, t, y_peers)
        spread(rb, rb_s, rb_r, t, zl, zl_peers)

    def sums_in(t):
        cols = gather(cb, cb_s, cb_r, t, zh_peers)
        rows = gather(rb, rb_s, rb_r, t, zl_peers)
        return rows, cols

    def duals_in(rowd, cold, step):
        tall = (step * cold).T
        for g in range(PROTOS // 128):
            wc[g * 16:(g + 1) * 16] = jnp.broadcast_to(tall[:, g:g + 1], (128, 128)).reshape(16, 8, 128)
        for l in range(LANES):
            wr[:, l * 128:(l + 1) * 128] = jnp.broadcast_to(step * rowd[l:l + 1, :], (8, 128))

    strides_in.wait()
    sigmas_in.wait()
    tau = [strides[t] / K for t in range(ROUNDS)]
    colacc[...] = jnp.zeros_like(colacc)
    rowacc[...] = jnp.zeros_like(rowacc)

    def unit_protos(h):
        protos_in(h).wait()
        for i in range(PHALF // 128):
            rows = slice(h * PHALF + i * 128, h * PHALF + (i + 1) * 128)
            uprot[rows, :] = unit_rows(protos[rows, :])

    def unit_points(j):
        pts_in(j).wait()
        rows = slice(j * PCHUNK, (j + 1) * PCHUNK)
        upts[rows, :] = unit_rows(pts[rows, :])

    def scores(first, count, lanes, width):
        rows = pl.ds(pl.multiple_of(first, BLOCK), count)
        groups = pl.ds(first // 8, count // 8)
        s = lax.dot_general(uprot[rows, :], upts[lanes, :], (((1,), (1,)), ((), ())), preferred_element_type=F32)
        s = s.reshape(count // 8, 8, width)
        a_ref[groups, :, lanes] = s
        p = jnp.maximum(s, 0.0)
        rowacc[:, lanes] += jnp.sum(p, axis=0)
        acc = p[:, :, 0:128]
        for l in range(1, width // 128):
            acc = acc + p[:, :, l * 128:(l + 1) * 128]
        colacc[groups] += acc

    unit_protos(0)
    unit_points(0)
    for j in range(NCHUNK):
        scores(0, PHALF, slice(j * PCHUNK, (j + 1) * PCHUNK), PCHUNK)
        if j + 1 < NCHUNK:
            unit_points(j + 1)
    unit_protos(1)

    def rest(i, carry):
        scores(i * BLOCK, BLOCK, slice(0, POINTS), POINTS)
        return carry

    lax.fori_loop(PHALF // BLOCK, ZH, rest, 0)
    pl.semaphore_wait(barrier, len(everyone))

    def first_plan(i, carry):
        rows = pl.ds(i * 4, 4)
        s = a_ref[rows]
        b_ref[rows] = jnp.maximum((tau[1] * scale) * s, ((tau[0] + tau[1]) * scale) * s)
        return carry

    def next_plan(i, carry):
        rows = pl.ds(i * 4, 4)
        b_ref[rows] = b_ref[rows] + (tau[2] * scale) * a_ref[rows]
        return carry

    def iterate(base, count, store):
        def step(i, carry):
            rows = pl.ds(base + i * 8, 8)
            c = wc[rows]
            acc = None
            for l in range(LANES):
                lanes = slice(l * 128, (l + 1) * 128)
                p = jnp.maximum(b_ref[rows, :, lanes] - (wr[:, lanes] + c), 0.0)
                rowacc[:, lanes] += jnp.sum(p, axis=0)
                acc = p if acc is None else acc + p
                store(i, rows, lanes, p)
            colacc[rows] = acc
            return carry

        lax.fori_loop(0, count, step, 0)

    sums_out(0, tau[0] * scale)
    lax.fori_loop(0, GROUPS // 8, first_plan, 0)
    sums_mid(0)
    lax.fori_loop(GROUPS // 8, GROUPS // 4, first_plan, 0)
    rows1, cols1 = sums_in(0)
    rowd = sigmas[0] * (2.0 * rows1 - 1.0)
    cold = sigmas[0] * (2.0 * cols1 - target)
    duals_in(rowd, cold, tau[1])

    rowacc[...] = jnp.zeros_like(rowacc)

    def keep(i, rows, lanes, p):
        b_ref[rows, :, lanes] = p

    iterate(0, GROUPS // 8, keep)
    sums_out(1, 1.0)
    lax.fori_loop(0, GROUPS // 8, next_plan, 0)
    sums_mid(1)
    lax.fori_loop(GROUPS // 8, GROUPS // 4, next_plan, 0)
    rows2, cols2 = sums_in(1)
    rowd = rowd + sigmas[1] * (2.0 * rows2 - rows1 - 1.0)
    cold = cold + sigmas[1] * (2.0 * cols2 - cols1 - target)
    duals_in(rowd, cold, tau[2])

    rowacc[...] = jnp.zeros_like(rowacc)
    other = 1 - core
    peer = at_xc(x * CORE + other)
    right, left, across = at_x(1), at_x(-1), at_x(2)
    up, down = at_zh(1), at_zh(-1)
    xp, xm, xo = (x + 1) % X, (x + X - 1) % X, (x + 2) % X
    lo, hi = pl.ds(0, HALF), pl.ds(HALF, HALF)

    def remote(src, dst, send, recv, index, dev):
        return pltpu.make_async_remote_copy(
            src_ref=src, dst_ref=dst, send_sem=send.at[index], recv_sem=recv.at[index],
            device_id=dev, device_id_type=MESH)

    def core_copy(c, h):
        return remote(part.at[c, h, :, other], corebuf.at[c, h], core_s, core_r, (c, h), peer)

    def x_copy(c, h, n):
        to, dev = ((xp, right), (xm, left), (xo, across))[n]
        return remote(part.at[c, h, to, core], xbuf.at[c, h, n], x_s, x_r, (c, h, n), dev)

    def far_copy(h, n):
        rows, dev = ((lo, up), (hi, down))[n]
        return remote(total.at[0, h, rows], zmid.at[h, n], far_s, far_r, (h, n), dev)

    def near_copy(h, n, second):
        rows = (lo, hi)[n if second else 1 - n]
        return remote(total.at[1 + n, h, rows], zend.at[h, n, rows], near_s, near_r, (h, n, int(second)), (up, down)[n])

    def over_h(step):
        def loop(h, carry):
            step(h)
            return carry

        lax.fori_loop(0, THIRDS, loop, 0)

    def x_out(c, h):
        core_copy(c, h).wait_recv()
        for n in (2, 0, 1):
            to = (xp, xm, xo)[n]
            part[c, h, to, core] += corebuf[c, h, to]
            x_copy(c, h, n).start()

    def x_in(c, h):
        for n in range(X - 1):
            x_copy(c, h, n).wait_recv()
        total[c, h] = part[c, h, x, core] + corebuf[c, h, x] + (xbuf[c, h, 0] + xbuf[c, h, 1] + xbuf[c, h, 2])

    def plan_block(c, carry):
        second, odd = c // 2, c % 2
        base = ((zh + 2 + second - odd + 2 * second * odd) % ZH) * BGROUPS

        def low(i, rows, lanes, p):
            plan[c, pl.ds(pl.multiple_of(i * 64, 64), 64), lanes] = p.reshape(64, 128).astype(BF16)

        iterate(base, BGROUPS // 8, low)
        return carry

    def sums_block(c, carry):
        def third(h):
            lanes = pl.ds(pl.multiple_of(h * 256, 256), 256)
            g = jnp.dot(plan[c], pts[:, lanes], preferred_element_type=F32)
            part[c, h] = g.reshape(X, CORE, OUT, 256)
            core_copy(c, h).start()

        over_h(third)
        return carry

    lax.fori_loop(0, 1, plan_block, 0)
    lax.fori_loop(0, 1, sums_block, 0)
    lax.fori_loop(1, ZH, plan_block, 0)
    sums_out(2, 1.0)
    over_h(lambda h: x_out(0, h))
    lax.fori_loop(1, 3, sums_block, 0)

    def both_out(h):
        x_out(1, h)
        x_out(2, h)

    over_h(both_out)
    lax.fori_loop(3, ZH, sums_block, 0)
    sums_mid(2)
    over_h(lambda h: x_out(3, h))

    def far_out(h):
        x_in(0, h)
        for n in range(2):
            far_copy(h, n).start()

    over_h(far_out)

    def near_out(h):
        x_in(1, h)
        near_copy(h, 0, False).start()
        x_in(2, h)
        near_copy(h, 1, False).start()
        for n in range(2):
            rows = (lo, hi)[n]
            far_copy(h, n).wait_recv()
            total[1 + n, h, rows] += zmid[h, n]
            near_copy(h, n, True).start()

    over_h(near_out)
    rows3, cols3 = sums_in(2)
    rowd_ref[...] = rowd + sigmas[2] * (2.0 * rows3 - rows2 - 1.0)
    cold_ref[...] = cold + sigmas[2] * (2.0 * cols3 - cols2 - target)
    count_ref[...] = cols3
    mine = count_ref[pl.ds(me_dp // 4, 1), :]
    sub = lax.broadcasted_iota(jnp.int32, (OUT, 128), 0)
    lane = lax.broadcasted_iota(jnp.int32, (OUT, 128), 1)
    counts = jnp.sum(jnp.where(lane == sub + (me_dp % 4) * OUT, mine, 0.0), axis=1, keepdims=True)
    over_h(lambda h: x_in(3, h))
    for h in range(THIRDS):
        lanes = slice(h * 256, (h + 1) * 256)
        for n in range(2):
            for second in (False, True):
                near_copy(h, n, second).wait_recv()
        gathered = total[3, h] + (zend[h, 0] + zend[h, 1])
        previous = protos[pl.ds(pl.multiple_of(me_dp * OUT, OUT), OUT), lanes].astype(F32)
        newp_ref[:, lanes] = (previous + gathered) / (1.0 + counts)

    def sent(h):
        def blocks(c, carry):
            core_copy(c, h).wait_send()
            for n in range(X - 1):
                x_copy(c, h, n).wait_send()
            return carry

        lax.fori_loop(0, ZH, blocks, 0)
        for n in range(2):
            far_copy(h, n).wait_send()
            near_copy(h, n, False).wait_send()
            near_copy(h, n, True).wait_send()

    over_h(sent)
    for copy in pending:
        copy.wait_send()


def results(rows_in, cols_in, new_in, rows_out, cols_out, new_out):
    rows_out[...] = rows_in[...]
    cols_out[...] = cols_in[...]
    new_out[...] = new_in[...]


def body(points, prototypes, plan_stride_lengths, sigma_steps):
    dma = pltpu.SemaphoreType.DMA
    vmem = pl.BlockSpec(memory_space=pltpu.VMEM)
    hbm = pl.BlockSpec(memory_space=pl.ANY)
    rows, cols, new = pl.pallas_call(
        kernel,
        out_shape=(
            jax.ShapeDtypeStruct((LANES, 128), F32),
            jax.ShapeDtypeStruct((PROTOS // 128, 128), F32),
            jax.ShapeDtypeStruct((OUT, WIDTH), F32),
        ),
        in_specs=[hbm, hbm, hbm, hbm],
        out_specs=(vmem, vmem, vmem),
        scratch_shapes=[
            pltpu.SMEM((ROUNDS,), F32),
            pltpu.SMEM((ROUNDS,), F32),
            pltpu.VMEM((POINTS, WIDTH), BF16),
            pltpu.VMEM((PROTOS, WIDTH), BF16),
            pltpu.VMEM((POINTS, WIDTH), BF16),
            pltpu.VMEM((PROTOS, WIDTH), BF16),
            pltpu.VMEM((GROUPS, 8, POINTS), F32),
            pltpu.VMEM((GROUPS, 8, POINTS), F32),
            pltpu.VMEM((ZH, BLOCK, POINTS), BF16),
            pltpu.VMEM((8, POINTS), F32),
            pltpu.VMEM((GROUPS, 8, 128), F32),
            pltpu.VMEM((8, POINTS), F32),
            pltpu.VMEM((GROUPS, 8, 128), F32),
            pltpu.VMEM((ROUNDS, Y, LANES, 128), F32),
            pltpu.VMEM((ROUNDS, ZL, LANES, 128), F32),
            pltpu.VMEM((ROUNDS, X * CORE, PROTOS // 128, 128), F32),
            pltpu.VMEM((ROUNDS, ZH, PROTOS // 128, 128), F32),
            pltpu.VMEM((ZH, THIRDS, X, CORE, OUT, 256), F32),
            pltpu.VMEM((ZH, THIRDS, X, OUT, 256), F32),
            pltpu.VMEM((ZH, THIRDS, X - 1, OUT, 256), F32),
            pltpu.VMEM((ZH, THIRDS, OUT, 256), F32),
            pltpu.VMEM((THIRDS, 2, HALF, 256), F32),
            pltpu.VMEM((THIRDS, 2, OUT, 256), F32),
            pltpu.VMEM((PROTOS // 128, 128), F32),
            dma((NCHUNK + 4,)),
            dma((ROUNDS, Y)), dma((ROUNDS, Y)),
            dma((ROUNDS, ZL)), dma((ROUNDS, ZL)),
            dma((ROUNDS, X * CORE)), dma((ROUNDS, X * CORE)),
            dma((ROUNDS, ZH)), dma((ROUNDS, ZH)),
            dma((ZH, THIRDS)), dma((ZH, THIRDS)),
            dma((ZH, THIRDS, X - 1)), dma((ZH, THIRDS, X - 1)),
            dma((THIRDS, 2)), dma((THIRDS, 2)),
            dma((THIRDS, 2, 2)), dma((THIRDS, 2, 2)),
        ],
        compiler_params=pltpu.CompilerParams(
            collective_id=0, has_side_effects=True, vmem_limit_bytes=56 * 1024 * 1024),
        name="assign",
    )(plan_stride_lengths, sigma_steps, points, prototypes)
    rows, cols, new = pl.pallas_call(
        results,
        out_shape=(
            jax.ShapeDtypeStruct((LANES, 128), F32),
            jax.ShapeDtypeStruct((PROTOS // 128, 128), F32),
            jax.ShapeDtypeStruct((OUT, WIDTH), F32),
        ),
        in_specs=[vmem, vmem, vmem],
        out_specs=(vmem, vmem, vmem),
        name="results",
    )(rows, cols, new)
    return rows.reshape(POINTS), cols.reshape(PROTOS), new


def solution(mesh):
    placed = (P("dp", None), P("proto", None), P(), P())
    return jax.shard_map(
        body,
        mesh=mesh,
        in_specs=placed,
        out_specs=(P("dp"), P("proto"), P(("proto", "dp"), None)),
        check_vma=False,
    )
```

time: 80.3 us -> 72.6 us (0.904)
  the two profiles are of different devices: /device:TPU:1 before, /device:TPU:64 now
where the time goes in v2:
time: 72.6 us; the launch traced here: 72.5 us
  Pallas kernels  71.8 us (99%)
    pallas_call x1, Pallas kernels, body(): pl.pallas_call(kernel, out_shape=(jax.ShapeDtypeStruct((LANES, 128), F32)...  70.2 us
    pallas_call x1, Pallas kernels, body(): pl.pallas_call(results, out_shape=(jax.ShapeDtypeStruct((LANES, 128), F32...  1.56 us

profile of v2, /device:TPU:64, one launch (start us, length us, event | category | flops | bytes accessed | tf_op | source)
XLA Modules:
  0.0 72.5 jit_solution(17937298614845917066)
XLA Ops:
  0.6 70.2 %assign.1 = (f32[16,128]{1,0:T(8,128)}, f32[8,128]{1,0:T(8,128)}, f32[32,768]{1,0:T(8,128)}) custom-call(f32[3]{0:T(128)} %strides_hbm.1, f32[3]{0:T(128)} %sigmas_hbm.1, bf16[2048,768]{1,0:T(8,128)(2,1)} %pts_hbm.1, bf16[1024,768]{1,0:T(8,128)(2,1)} %protos_hbm.1), custom_call_target="tpu_custom_call" | custom-call | tf_op jit(solution)/shard_map/assign/pallas_call | solution.py:386
  70.9 1.6 %results.1 = (f32[16,128]{1,0:T(8,128)}, f32[8,128]{1,0:T(8,128)}, f32[32,768]{1,0:T(8,128)}) custom-call(f32[16,128]{1,0:T(8,128)} %get-tuple-element.9.rows_in, f32[8,128]{1,0:T(8,128)} %get-tuple-element.10.cols_in, f32[32,768]{1,0:T(8,128)} %get-tuple-element.11.new_in), custom_call_target="tpu_custom_call" | custom-call | tf_op jit(solution)/shard_map/results/pallas_call | solution.py:434

commit v3 on v2

--- a/solution.py
+++ b/solution.py
@@ -34,8 +34,8 @@
     strides_hbm, sigmas_hbm, pts_hbm, protos_hbm,
     rowd_ref, cold_ref, newp_ref,
     strides, sigmas, pts, protos, upts, uprot, a_ref, b_ref, plan, wr, wc, rowacc, colacc,
-    ra, rb, ca, cb, part, corebuf, xbuf, total, zmid, zend, count_ref,
-    in_sem, ra_s, ra_r, rb_s, rb_r, ca_s, ca_r, cb_s, cb_r, core_s, core_r, x_s, x_r, far_s, far_r, near_s, near_r,
+    ra, rb, ca, cf, cb, part, corebuf, xbuf, total, zmid, zend, count_ref,
+    in_sem, ra_s, ra_r, rb_s, rb_r, ca_s, ca_r, cf_s, cf_r, cb_s, cb_r, core_s, core_r, x_s, x_r, far_s, far_r, near_s, near_r,
 ):
     me_dp, me_pr = lax.axis_index("dp"), lax.axis_index("proto")
     zh, x, core = me_dp // (X * CORE), (me_dp // CORE) % X, me_dp % CORE
@@ -61,10 +61,14 @@
     for d in range(1, X * CORE):
         slot = ((x + d // CORE) % X) * CORE + (core + d % CORE) % CORE
         xc_peers.append((slot, at_xc(slot)))
-    zh_peers = [((zh + d) % ZH, at_zh(d)) for d in range(1, ZH)]
+    far_peers = []
+    for d in range(X * CORE):
+        slot = ((x + d // CORE) % X) * CORE + (core + d % CORE) % CORE
+        far_peers.append((slot, (((zh + 2) % ZH) * (X * CORE) + slot, me_pr)))
+    zh_peers = [((zh + d) % ZH, at_zh(d)) for d in (1, ZH - 1)]
     y_peers = [((y + d) % Y, at_y(d)) for d in range(1, Y)]
     zl_peers = [((zl + d) % ZL, at_zl(d)) for d in range(1, ZL)]
-    everyone = xc_peers + zh_peers + y_peers + zl_peers
+    everyone = xc_peers + far_peers + zh_peers + y_peers + zl_peers
 
     barrier = pltpu.get_barrier_semaphore()
     for _, dev in everyone:
@@ -101,21 +105,34 @@
             copy.start()
             pending.append(copy)
 
+    def far_group(t, slot, dev):
+        return pltpu.make_async_remote_copy(
+            src_ref=ca.at[t, xc], dst_ref=cf.at[t, xc],
+            send_sem=cf_s.at[t, slot], recv_sem=cf_r.at[t, xc],
+            device_id=dev, device_id_type=MESH)
+
+    def total_of(buf, t):
+        out = buf[t, 0]
+        for slot in range(1, buf.shape[1]):
+            out = out + buf[t, slot]
+        return out
+
     def gather(buf, send, recv, t, peers):
         for slot, dev in peers:
             pltpu.make_async_remote_copy(
                 src_ref=buf.at[t, slot], dst_ref=buf.at[t, slot],
                 send_sem=send.at[t, slot], recv_sem=recv.at[t, slot],
                 device_id=dev, device_id_type=MESH).wait_recv()
-        out = buf[t, 0]
-        for slot in range(1, buf.shape[1]):
-            out = out + buf[t, slot]
-        return out
+        return total_of(buf, t)
 
     def sums_out(t, factor):
         for g in range(PROTOS // 128):
             block = colacc[g * 16:(g + 1) * 16].reshape(128, 128)
             ca[t, xc, g:g + 1, :] = factor * jnp.sum(block.T, axis=0, keepdims=True)
+        for slot, dev in far_peers:
+            copy = far_group(t, slot, dev)
+            copy.start()
+            pending.append(copy)
         spread(ca, ca_s, ca_r, t, xc, xc_peers)
         for l in range(LANES):
             ra[t, y, l:l + 1, :] = factor * jnp.sum(rowacc[:, l * 128:(l + 1) * 128], axis=0, keepdims=True)
@@ -127,17 +144,26 @@
         rb[t, zl] = gather(ra, ra_s, ra_r, t, y_peers)
         spread(rb, rb_s, rb_r, t, zl, zl_peers)
 
-    def sums_in(t):
-        cols = gather(cb, cb_s, cb_r, t, zh_peers)
-        rows = gather(rb, rb_s, rb_r, t, zl_peers)
-        return rows, cols
-
-    def duals_in(rowd, cold, step):
+    def rows_in(t):
+        return gather(rb, rb_s, rb_r, t, zl_peers)
+
+    def cols_in(t):
+        for slot, dev in far_peers:
+            pltpu.make_async_remote_copy(
+                src_ref=ca.at[t, xc], dst_ref=cf.at[t, slot],
+                send_sem=cf_s.at[t, slot], recv_sem=cf_r.at[t, slot],
+                device_id=dev, device_id_type=MESH).wait_recv()
+        cb[t, (zh + 2) % ZH] = total_of(cf, t)
+        return gather(cb, cb_s, cb_r, t, zh_peers)
+
+    def rowd_in(rowd, step):
+        for l in range(LANES):
+            wr[:, l * 128:(l + 1) * 128] = jnp.broadcast_to(step * rowd[l:l + 1, :], (8, 128))
+
+    def cold_in(cold, step):
         tall = (step * cold).T
         for g in range(PROTOS // 128):
             wc[g * 16:(g + 1) * 16] = jnp.broadcast_to(tall[:, g:g + 1], (128, 128)).reshape(16, 8, 128)
-        for l in range(LANES):
-            wr[:, l * 128:(l + 1) * 128] = jnp.broadcast_to(step * rowd[l:l + 1, :], (8, 128))
 
     strides_in.wait()
     sigmas_in.wait()
@@ -215,12 +241,14 @@
     lax.fori_loop(0, GROUPS // 8, first_plan, 0)
     sums_mid(0)
     lax.fori_loop(GROUPS // 8, GROUPS // 4, first_plan, 0)
-    rows1, cols1 = sums_in(0)
+    rowacc[...] = jnp.zeros_like(rowacc)
+    rows1 = rows_in(0)
     rowd = sigmas[0] * (2.0 * rows1 - 1.0)
+    rowd_in(rowd, tau[1])
+    cols1 = cols_in(0)
     cold = sigmas[0] * (2.0 * cols1 - target)
-    duals_in(rowd, cold, tau[1])
-
-    rowacc[...] = jnp.zeros_like(rowacc)
+    cold_in(cold, tau[1])
+
 
     def keep(i, rows, lanes, p):
         b_ref[rows, :, lanes] = p
@@ -230,12 +258,14 @@
     lax.fori_loop(0, GROUPS // 8, next_plan, 0)
     sums_mid(1)
     lax.fori_loop(GROUPS // 8, GROUPS // 4, next_plan, 0)
-    rows2, cols2 = sums_in(1)
+    rowacc[...] = jnp.zeros_like(rowacc)
+    rows2 = rows_in(1)
     rowd = rowd + sigmas[1] * (2.0 * rows2 - rows1 - 1.0)
+    rowd_in(rowd, tau[2])
+    cols2 = cols_in(1)
     cold = cold + sigmas[1] * (2.0 * cols2 - cols1 - target)
-    duals_in(rowd, cold, tau[2])
-
-    rowacc[...] = jnp.zeros_like(rowacc)
+    cold_in(cold, tau[2])
+
     other = 1 - core
     peer = at_xc(x * CORE + other)
     right, left, across = at_x(1), at_x(-1), at_x(2)
@@ -304,32 +334,42 @@
 
     lax.fori_loop(0, 1, plan_block, 0)
     lax.fori_loop(0, 1, sums_block, 0)
-    lax.fori_loop(1, ZH, plan_block, 0)
+    lax.fori_loop(1, 2, plan_block, 0)
+    x_out(0, 0)
+    x_out(0, 1)
+    lax.fori_loop(2, ZH, plan_block, 0)
     sums_out(2, 1.0)
-    over_h(lambda h: x_out(0, h))
+    x_out(0, 2)
     lax.fori_loop(1, 3, sums_block, 0)
-
-    def both_out(h):
-        x_out(1, h)
-        x_out(2, h)
-
-    over_h(both_out)
+    x_out(1, 0)
+    x_out(2, 0)
+    x_out(1, 1)
     lax.fori_loop(3, ZH, sums_block, 0)
-    sums_mid(2)
-    over_h(lambda h: x_out(3, h))
 
     def far_out(h):
         x_in(0, h)
         for n in range(2):
             far_copy(h, n).start()
+        x_out(2 - h % 2, 1 + (h + 1) // 2)
 
     over_h(far_out)
+    sums_mid(2)
 
     def near_out(h):
         x_in(1, h)
         near_copy(h, 0, False).start()
+
+        @pl.when(h < 2)
+        def _():
+            x_out(3, 2 * h)
+
         x_in(2, h)
         near_copy(h, 1, False).start()
+
+        @pl.when(h == 0)
+        def _():
+            x_out(3, 1)
+
         for n in range(2):
             rows = (lo, hi)[n]
             far_copy(h, n).wait_recv()
@@ -337,7 +377,9 @@
             near_copy(h, n, True).start()
 
     over_h(near_out)
-    rows3, cols3 = sums_in(2)
+    over_h(lambda h: x_in(3, h))
+    rows3 = rows_in(2)
+    cols3 = cols_in(2)
     rowd_ref[...] = rowd + sigmas[2] * (2.0 * rows3 - rows2 - 1.0)
     cold_ref[...] = cold + sigmas[2] * (2.0 * cols3 - cols2 - target)
     count_ref[...] = cols3
@@ -345,7 +387,6 @@
     sub = lax.broadcasted_iota(jnp.int32, (OUT, 128), 0)
     lane = lax.broadcasted_iota(jnp.int32, (OUT, 128), 1)
     counts = jnp.sum(jnp.where(lane == sub + (me_dp % 4) * OUT, mine, 0.0), axis=1, keepdims=True)
-    over_h(lambda h: x_in(3, h))
     for h in range(THIRDS):
         lanes = slice(h * 256, (h + 1) * 256)
         for n in range(2):
@@ -409,6 +450,7 @@
             pltpu.VMEM((ROUNDS, Y, LANES, 128), F32),
             pltpu.VMEM((ROUNDS, ZL, LANES, 128), F32),
             pltpu.VMEM((ROUNDS, X * CORE, PROTOS // 128, 128), F32),
+            pltpu.VMEM((ROUNDS, X * CORE, PROTOS // 128, 128), F32),
             pltpu.VMEM((ROUNDS, ZH, PROTOS // 128, 128), F32),
             pltpu.VMEM((ZH, THIRDS, X, CORE, OUT, 256), F32),
             pltpu.VMEM((ZH, THIRDS, X, OUT, 256), F32),
@@ -420,6 +462,7 @@
             dma((NCHUNK + 4,)),
             dma((ROUNDS, Y)), dma((ROUNDS, Y)),
             dma((ROUNDS, ZL)), dma((ROUNDS, ZL)),
+            dma((ROUNDS, X * CORE)), dma((ROUNDS, X * CORE)),
             dma((ROUNDS, X * CORE)), dma((ROUNDS, X * CORE)),
             dma((ROUNDS, ZH)), dma((ROUNDS, ZH)),
             dma((ZH, THIRDS)), dma((ZH, THIRDS)),

time: 72.6 us -> 69.7 us (0.960)
  the two profiles are of different devices: /device:TPU:64 before, /device:TPU:1 now
where the time goes in v3:
time: 69.7 us; the launch traced here: 69.6 us
  Pallas kernels  68.9 us (99%)
    pallas_call x1, Pallas kernels, body(): pl.pallas_call(kernel, out_shape=(jax.ShapeDtypeStruct((LANES, 128), F32)...  67.4 us
    pallas_call x1, Pallas kernels, body(): pl.pallas_call(results, out_shape=(jax.ShapeDtypeStruct((LANES, 128), F32...  1.56 us

profile of v3, /device:TPU:1, one launch (start us, length us, event | category | flops | bytes accessed | tf_op | source)
XLA Modules:
  0.0 69.6 jit_solution(2215708663741153545)
XLA Ops:
  0.6 67.4 %assign.1 = (f32[16,128]{1,0:T(8,128)}, f32[8,128]{1,0:T(8,128)}, f32[32,768]{1,0:T(8,128)}) custom-call(f32[3]{0:T(128)} %strides_hbm.1, f32[3]{0:T(128)} %sigmas_hbm.1, bf16[2048,768]{1,0:T(8,128)(2,1)} %pts_hbm.1, bf16[1024,768]{1,0:T(8,128)(2,1)} %protos_hbm.1), custom_call_target="tpu_custom_call" | custom-call | tf_op jit(solution)/shard_map/assign/pallas_call | solution.py:427
  68.0 1.6 %results.1 = (f32[16,128]{1,0:T(8,128)}, f32[8,128]{1,0:T(8,128)}, f32[32,768]{1,0:T(8,128)}) custom-call(f32[16,128]{1,0:T(8,128)} %get-tuple-element.9.rows_in, f32[8,128]{1,0:T(8,128)} %get-tuple-element.10.cols_in, f32[32,768]{1,0:T(8,128)} %get-tuple-element.11.new_in), custom_call_target="tpu_custom_call" | custom-call | tf_op jit(solution)/shard_map/results/pallas_call | solution.py:477

commit v4 on v3

--- a/solution.py
+++ b/solution.py
@@ -222,20 +222,23 @@
         return carry
 
     def iterate(base, count, store):
-        def step(i, carry):
+        def step(i, sums):
             rows = pl.ds(base + i * 8, 8)
             c = wc[rows]
-            acc = None
+            acc, out = None, []
             for l in range(LANES):
                 lanes = slice(l * 128, (l + 1) * 128)
                 p = jnp.maximum(b_ref[rows, :, lanes] - (wr[:, lanes] + c), 0.0)
-                rowacc[:, lanes] += jnp.sum(p, axis=0)
+                out.append(sums[l] + jnp.sum(p, axis=0))
                 acc = p if acc is None else acc + p
                 store(i, rows, lanes, p)
             colacc[rows] = acc
-            return carry
-
-        lax.fori_loop(0, count, step, 0)
+            return tuple(out)
+
+        none = tuple(jnp.zeros((8, 128), F32) for _ in range(LANES))
+        sums = lax.fori_loop(0, count, step, none)
+        for l in range(LANES):
+            rowacc[:, l * 128:(l + 1) * 128] += sums[l]
 
     sums_out(0, tau[0] * scale)
     lax.fori_loop(0, GROUPS // 8, first_plan, 0)
@@ -322,14 +325,14 @@
         iterate(base, BGROUPS // 8, low)
         return carry
 
+    def third(c, h):
+        lanes = pl.ds(pl.multiple_of(h * 256, 256), 256)
+        g = jnp.dot(plan[c], pts[:, lanes], preferred_element_type=F32)
+        part[c, h] = g.reshape(X, CORE, OUT, 256)
+        core_copy(c, h).start()
+
     def sums_block(c, carry):
-        def third(h):
-            lanes = pl.ds(pl.multiple_of(h * 256, 256), 256)
-            g = jnp.dot(plan[c], pts[:, lanes], preferred_element_type=F32)
-            part[c, h] = g.reshape(X, CORE, OUT, 256)
-            core_copy(c, h).start()
-
-        over_h(third)
+        over_h(lambda h: third(c, h))
         return carry
 
     lax.fori_loop(0, 1, plan_block, 0)
@@ -344,13 +347,13 @@
     x_out(1, 0)
     x_out(2, 0)
     x_out(1, 1)
-    lax.fori_loop(3, ZH, sums_block, 0)
 
     def far_out(h):
         x_in(0, h)
         for n in range(2):
             far_copy(h, n).start()
         x_out(2 - h % 2, 1 + (h + 1) // 2)
+        third(3, h)
 
     over_h(far_out)
     sums_mid(2)
@@ -427,9 +430,9 @@
     rows, cols, new = pl.pallas_call(
         kernel,
         out_shape=(
-            jax.ShapeDtypeStruct((LANES, 128), F32),
-            jax.ShapeDtypeStruct((PROTOS // 128, 128), F32),
-            jax.ShapeDtypeStruct((OUT, WIDTH), F32),
+            pltpu.VMEM((LANES, 128), F32),
+            pltpu.VMEM((PROTOS // 128, 128), F32),
+            pltpu.VMEM((OUT, WIDTH), F32),
         ),
         in_specs=[hbm, hbm, hbm, hbm],
         out_specs=(vmem, vmem, vmem),
@@ -483,6 +486,7 @@
         ),
         in_specs=[vmem, vmem, vmem],
         out_specs=(vmem, vmem, vmem),
+        compiler_params=pltpu.CompilerParams(vmem_limit_bytes=2 * 1024 * 1024),
         name="results",
     )(rows, cols, new)
     return rows.reshape(POINTS), cols.reshape(PROTOS), new

time: 69.7 us -> 66.6 us (0.956); the launches traced: 69.6 us -> 65.4 us
  Pallas kernels: 68.9 us -> 64.8 us
    pallas_call x1, Pallas kernels: 67.4 us -> 64.1 us  [body(): pl.pallas_call(kernel, out_shape=(pltpu.VMEM((LANES, 128), F32), pltpu.VM...]
    pallas_call x1, Pallas kernels: 1.56 us -> 0.66 us  [body(): pl.pallas_call(results, out_shape=(jax.ShapeDtypeStruct((LANES, 128), F32...]
where the time goes in v4:
time: 66.6 us; the launch traced here: 65.4 us
  Pallas kernels  64.8 us (97%)
    pallas_call x1, Pallas kernels, body(): pl.pallas_call(kernel, out_shape=(pltpu.VMEM((LANES, 128), F32), pltpu.VM...  64.1 us

profile of v4, /device:TPU:1, one launch (start us, length us, event | category | flops | bytes accessed | tf_op | source)
XLA Modules:
  0.0 65.4 jit_solution(10789902319156845297)
XLA Ops:
  0.6 64.1 %assign.1 = (f32[16,128]{1,0:T(8,128)S(1)}, f32[8,128]{1,0:T(8,128)S(1)}, f32[32,768]{1,0:T(8,128)S(1)}) custom-call(f32[3]{0:T(128)} %strides_hbm.1, f32[3]{0:T(128)} %sigmas_hbm.1, bf16[2048,768]{1,0:T(8,128)(2,1)} %pts_hbm.1, bf16[1024,768]{1,0:T(8,128)(2,1)} %protos_hbm.1), custom_call_target="tpu_custom_call" | custom-call | tf_op jit(solution)/shard_map/assign/pallas_call | solution.py:430
  64.8 0.7 %results.1 = (f32[16,128]{1,0:T(8,128)}, f32[8,128]{1,0:T(8,128)}, f32[32,768]{1,0:T(8,128)}) custom-call(f32[16,128]{1,0:T(8,128)S(1)} %get-tuple-element.9.rows_in, f32[8,128]{1,0:T(8,128)S(1)} %get-tuple-element.10.cols_in, f32[32,768]{1,0:T(8,128)S(1)} %get-tuple-element.11.new_in), custom_call_target="tpu_custom_call" | custom-call | tf_op jit(solution)/shard_map/results/pallas_call | solution.py:480

commit v5 on v4

--- a/solution.py
+++ b/solution.py
@@ -14,7 +14,7 @@
 POINTS, PROTOS, WIDTH = 2048, 1024, 768
 PCHUNK = 512
 NCHUNK = POINTS // PCHUNK
-PHALF = PROTOS // 2
+PFIRST = PROTOS * 3 // 4
 LANES = POINTS // 128
 GROUPS = PROTOS // 8
 BLOCK = PROTOS // ZH
@@ -74,18 +74,21 @@
     for _, dev in everyone:
         pl.semaphore_signal(barrier, inc=1, device_id=dev, device_id_type=MESH)
 
-    def protos_in(h):
-        rows = pl.ds(h * PHALF, PHALF)
-        return pltpu.make_async_copy(protos_hbm.at[rows], protos.at[rows], in_sem.at[NCHUNK + h])
+    def protos_in(first, count, sem):
+        rows = pl.ds(first, count)
+        return pltpu.make_async_copy(protos_hbm.at[rows], protos.at[rows], in_sem.at[sem])
+
+    protos_first = protos_in(0, PFIRST, NCHUNK)
+    protos_rest = protos_in(PFIRST, PROTOS - PFIRST, NCHUNK + 1)
 
     def pts_in(j):
         rows = pl.ds(j * PCHUNK, PCHUNK)
         return pltpu.make_async_copy(pts_hbm.at[rows], pts.at[rows], in_sem.at[j])
 
-    protos_in(0).start()
+    protos_first.start()
     for j in range(NCHUNK):
         pts_in(j).start()
-    protos_in(1).start()
+    protos_rest.start()
     strides_in = pltpu.make_async_copy(strides_hbm, strides, in_sem.at[NCHUNK + 2])
     sigmas_in = pltpu.make_async_copy(sigmas_hbm, sigmas, in_sem.at[NCHUNK + 3])
     strides_in.start()
@@ -171,10 +174,10 @@
     colacc[...] = jnp.zeros_like(colacc)
     rowacc[...] = jnp.zeros_like(rowacc)
 
-    def unit_protos(h):
-        protos_in(h).wait()
-        for i in range(PHALF // 128):
-            rows = slice(h * PHALF + i * 128, h * PHALF + (i + 1) * 128)
+    def unit_protos(copy, first, count):
+        copy.wait()
+        for i in range(count // 128):
+            rows = slice(first + i * 128, first + (i + 1) * 128)
             uprot[rows, :] = unit_rows(protos[rows, :])
 
     def unit_points(j):
@@ -195,19 +198,19 @@
             acc = acc + p[:, :, l * 128:(l + 1) * 128]
         colacc[groups] += acc
 
-    unit_protos(0)
+    unit_protos(protos_first, 0, PFIRST)
     unit_points(0)
     for j in range(NCHUNK):
-        scores(0, PHALF, slice(j * PCHUNK, (j + 1) * PCHUNK), PCHUNK)
+        scores(0, PFIRST, slice(j * PCHUNK, (j + 1) * PCHUNK), PCHUNK)
         if j + 1 < NCHUNK:
             unit_points(j + 1)
-    unit_protos(1)
+    unit_protos(protos_rest, PFIRST, PROTOS - PFIRST)
 
     def rest(i, carry):
         scores(i * BLOCK, BLOCK, slice(0, POINTS), POINTS)
         return carry
 
-    lax.fori_loop(PHALF // BLOCK, ZH, rest, 0)
+    lax.fori_loop(PFIRST // BLOCK, ZH, rest, 0)
     pl.semaphore_wait(barrier, len(everyone))
 
     def first_plan(i, carry):

time: 66.6 us -> 67.5 us (1.014); the launches traced: 65.4 us -> 67.3 us
  Pallas kernels: 64.8 us -> 66.7 us
    pallas_call x1, Pallas kernels: 64.1 us -> 66 us  [body(): pl.pallas_call(kernel, out_shape=(pltpu.VMEM((LANES, 128), F32), pltpu.VM...]
where the time goes in v5:
time: 67.5 us; the launch traced here: 67.3 us
  Pallas kernels  66.7 us (99%)
    pallas_call x1, Pallas kernels, body(): pl.pallas_call(kernel, out_shape=(pltpu.VMEM((LANES, 128), F32), pltpu.VM...  66 us

profile of v5, /device:TPU:1, one launch (start us, length us, event | category | flops | bytes accessed | tf_op | source)
XLA Modules:
  0.0 67.3 jit_solution(10460054329000680842)
XLA Ops:
  0.6 66.0 %assign.1 = (f32[16,128]{1,0:T(8,128)S(1)}, f32[8,128]{1,0:T(8,128)S(1)}, f32[32,768]{1,0:T(8,128)S(1)}) custom-call(f32[3]{0:T(128)} %strides_hbm.1, f32[3]{0:T(128)} %sigmas_hbm.1, bf16[2048,768]{1,0:T(8,128)(2,1)} %pts_hbm.1, bf16[1024,768]{1,0:T(8,128)(2,1)} %protos_hbm.1), custom_call_target="tpu_custom_call" | custom-call | tf_op jit(solution)/shard_map/assign/pallas_call | solution.py:433
  66.7 0.7 results.1
